TPU v7x, 32 devices: a whole 2x2x4 slice. The times are simulated.
32 devices in a mesh: dp: 8 (over z, x), seq: 4 (over y, core).
Axes of the slice: x: 2, y: 2, z: 4, core: 2. Of those that a mesh axis runs over, the one named last changes fastest.
Arguments:
- tokens: bfloat16 [64, 512, 768], P('dp', 'seq'), may hold values from -6 to 6
- cotangent: bfloat16 [64, 512, 768], P('dp', 'seq'), may hold values from -6 to 6
- segments: int32 [64, 512], P('dp', 'seq'), may hold values from 0 to 3, as said below
- w_query: bfloat16 [768, 768], replicated, may hold values from -0.21875 to 0.21875
- b_query: bfloat16 [768], replicated, may hold values from -4 to 4
- w_key: bfloat16 [768, 768], replicated, may hold values from -0.21875 to 0.21875
- w_value: bfloat16 [768, 768], replicated, may hold values from -0.21875 to 0.21875
- b_value: bfloat16 [768], replicated, may hold values from -4 to 4
- w_out: bfloat16 [768, 768], replicated, may hold values from -1.75 to 1.75
- b_out: bfloat16 [768], replicated, may hold values from -4 to 4
- gain_one: bfloat16 [768], replicated, may hold values from 0.5 to 1.5
- shift_one: bfloat16 [768], replicated, may hold values from -4 to 4
- w_inner: bfloat16 [768, 3072], replicated, may hold values from -0.21875 to 0.21875
- b_inner: bfloat16 [3072], replicated, may hold values from -4 to 4
- w_outer: bfloat16 [3072, 768], replicated, may hold values from -0.109375 to 0.109375
- b_outer: bfloat16 [768], replicated, may hold values from -4 to 4
- gain_two: bfloat16 [768], replicated, may hold values from 0.5 to 1.5
- shift_two: bfloat16 [768], replicated, may hold values from -4 to 4
Outputs:
- output: bfloat16 [64, 512, 768], P('dp', 'seq')
- grad_tokens: bfloat16 [64, 512, 768], P('dp', 'seq')
- grad_w_query: float32 [768, 768], P('dp', 'seq')
- grad_b_query: float32 [768], P('dp')
- grad_w_key: float32 [768, 768], P('dp', 'seq')
- grad_w_value: float32 [768, 768], P('dp', 'seq')
- grad_b_value: float32 [768], P('dp')
- grad_w_out: float32 [768, 768], P('dp', 'seq')
- grad_b_out: float32 [768], P('dp')
- grad_gain_one: float32 [768], P('dp')
- grad_shift_one: float32 [768], P('dp')
- grad_w_inner: float32 [768, 3072], P('dp', 'seq')
- grad_b_inner: float32 [3072], P('dp')
- grad_w_outer: float32 [3072, 768], P('dp', 'seq')
- grad_b_outer: float32 [768], P('dp')
- grad_gain_two: float32 [768], P('dp')
- grad_shift_two: float32 [768], P('dp')
Inputs may be any that keep to these rules, and one draw needn't show every extreme that they name: `segments`: in each row, ids never fall except to 0: an optional fragment 1, then fragment 2, which starts within the row's first 128 tokens and ends within its last 128, then fragment 3, then padding 0 up to the row's end.
All inputs are finite; a program needn't handle non-finite values.
Results may differ from a plain program's by a relative error of at most 0.019.
Values may be sent and summed in bfloat16 or wider, within the bound.
No kernel may reach another device: no remote copies, remote signals or barrier semaphores. Data moves between devices by JAX's collectives and lax.ppermute only.
A program may use at most 192 MiB of HBM per device.

v0:
```python
import jax
import jax.numpy as jnp
from jax import lax
from jax.sharding import PartitionSpec as P

HEADS = 12
ROWS_MB = 2
MICRO = 4


def as_sent(array):
    return jax.tree.map(lambda a: a.astype(jnp.bfloat16) if a.dtype == jnp.float32 else a, array)


def layer_norm(values, gain, shift):
    centred = values - jnp.mean(values, -1, keepdims=True)
    inverse = lax.rsqrt(jnp.mean(centred * centred, -1, keepdims=True) + 1e-05)
    normed = centred * inverse
    return (normed * gain.astype(jnp.float32) + shift.astype(jnp.float32), normed, inverse)


def norm_back(upstream, normed, inverse, gain):
    scaled = upstream * gain.astype(jnp.float32)
    return inverse * (
        scaled
        - jnp.mean(scaled, -1, keepdims=True)
        - normed * jnp.mean(scaled * normed, -1, keepdims=True)
    )


def gelu_value(values):
    return 0.5 * values * (1.0 + jax.scipy.special.erf(values * 0.7071067811865476))


def gelu_slope(values):
    return (
        0.5 * (1.0 + jax.scipy.special.erf(values * 0.7071067811865476))
        + values * jnp.exp(-0.5 * values * values) * 0.3989422804014327
    )


def matmul(pattern, left, right):
    return jnp.einsum(pattern, left, right, preferred_element_type=jnp.float32)


def column_sum(values):
    return jnp.sum(values.astype(jnp.float32), 0)


def split_heads(values, rows, length):
    head_dim = values.shape[-1] // HEADS
    return (
        values.reshape(rows, length, HEADS, head_dim)
        .transpose(0, 2, 1, 3)
        .reshape(rows * HEADS, length, head_dim)
    )


def join_heads(values, rows, length):
    head_dim = values.shape[-1]
    return (
        values.reshape(rows, HEADS, length, head_dim)
        .transpose(0, 2, 1, 3)
        .reshape(rows * length, HEADS * head_dim)
    )


def body(
    tokens,
    cotangent,
    segments,
    w_query,
    b_query,
    w_key,
    w_value,
    b_value,
    w_out,
    b_out,
    gain_one,
    shift_one,
    w_inner,
    b_inner,
    w_outer,
    b_outer,
    gain_two,
    shift_two,
):
    groups = lax.axis_size("seq")
    place = lax.axis_index("seq")
    rows_dev, local, width = tokens.shape
    head_dim = width // HEADS
    scale = head_dim ** (-0.5)

    def masked_scores(query, keys, masking):
        raw = matmul("pqd,pkd->pqk", query, keys) * scale
        return jnp.where(masking, raw, -1e30)

    running = None
    pairs = ROWS_MB * HEADS // groups
    fragments_all = lax.all_gather(segments, "seq", axis=1, tiled=True)
    pair_rows = (place * pairs + jnp.arange(pairs, dtype=jnp.int32)) // HEADS

    def heads_grads_out(grad_query, grad_keys, grad_values):
        moved = (
            lax.all_to_all(grad_query, "seq", split_axis=1, concat_axis=0, tiled=True),
            lax.all_to_all(grad_keys, "seq", split_axis=1, concat_axis=0, tiled=True),
            lax.all_to_all(grad_values, "seq", split_axis=1, concat_axis=0, tiled=True),
        )
        return tuple((join_heads(piece, ROWS_MB, local) for piece in moved))

    results = []
    input_grads = []
    for micro in range(MICRO):
        first = micro * ROWS_MB
        inputs = tokens[first : first + ROWS_MB].reshape(ROWS_MB * local, width)
        upstream = (
            cotangent[first : first + ROWS_MB].reshape(ROWS_MB * local, width).astype(jnp.float32)
        )
        fragment_pairs = jnp.take(fragments_all[first : first + ROWS_MB], pair_rows, axis=0)
        masking = fragment_pairs[:, :, None] == fragment_pairs[:, None, :]
        projections_query = (
            jnp.dot(inputs, w_query, preferred_element_type=jnp.float32) + b_query
        ).astype(jnp.bfloat16)
        projections_keys = jnp.dot(inputs, w_key, preferred_element_type=jnp.float32).astype(
            jnp.bfloat16
        )
        projections_values = (
            jnp.dot(inputs, w_value, preferred_element_type=jnp.float32) + b_value
        ).astype(jnp.bfloat16)
        query_h = lax.all_to_all(
            split_heads(projections_query, ROWS_MB, local),
            "seq",
            split_axis=0,
            concat_axis=1,
            tiled=True,
        )
        keys_h = lax.all_to_all(
            split_heads(projections_keys, ROWS_MB, local),
            "seq",
            split_axis=0,
            concat_axis=1,
            tiled=True,
        )
        values_h = lax.all_to_all(
            split_heads(projections_values, ROWS_MB, local),
            "seq",
            split_axis=0,
            concat_axis=1,
            tiled=True,
        )
        scores = masked_scores(query_h, keys_h, masking)
        highest = jnp.max(scores, -1, keepdims=True)
        expo = jnp.exp(scores - highest)
        totals = jnp.sum(expo, -1, keepdims=True)
        prob = expo / totals
        log_total = highest + jnp.log(totals)
        layer_context = matmul("pqk,pkd->pqd", prob.astype(jnp.bfloat16), values_h).astype(
            jnp.bfloat16
        )
        context_tok = join_heads(
            lax.all_to_all(layer_context, "seq", split_axis=1, concat_axis=0, tiled=True),
            ROWS_MB,
            local,
        )
        resid_one = (
            inputs.astype(jnp.float32)
            + jnp.dot(context_tok, w_out, preferred_element_type=jnp.float32)
            + b_out
        )
        hidden_one, normed_one, inverse_one = layer_norm(resid_one, gain_one, shift_one)
        hidden_low = hidden_one.astype(jnp.bfloat16)
        inner = jnp.dot(hidden_low, w_inner, preferred_element_type=jnp.float32) + b_inner
        active = gelu_value(inner).astype(jnp.bfloat16)
        resid_two = (
            hidden_one + jnp.dot(active, w_outer, preferred_element_type=jnp.float32) + b_outer
        )
        result, normed_two, inverse_two = layer_norm(resid_two, gain_two, shift_two)
        grad_gain_two = jnp.sum(upstream * normed_two, 0)
        grad_shift_two = jnp.sum(upstream, 0)
        grad_resid_two = norm_back(upstream, normed_two, inverse_two, gain_two)
        grad_branch = grad_resid_two.astype(jnp.bfloat16)
        grad_b_outer = column_sum(grad_branch)
        grad_w_outer = matmul("nf,nd->fd", active, grad_branch)
        grad_inner = (matmul("nd,fd->nf", grad_branch, w_outer) * gelu_slope(inner)).astype(
            jnp.bfloat16
        )
        grad_b_inner = column_sum(grad_inner)
        grad_w_inner = matmul("nd,nf->df", hidden_low, grad_inner)
        grad_hidden = grad_resid_two + matmul("nf,df->nd", grad_inner, w_inner)
        grad_gain_one = jnp.sum(grad_hidden * normed_one, 0)
        grad_shift_one = jnp.sum(grad_hidden, 0)
        grad_resid_one = norm_back(grad_hidden, normed_one, inverse_one, gain_one)
        grad_attn = grad_resid_one.astype(jnp.bfloat16)
        grad_b_out = column_sum(grad_attn)
        grad_w_out = matmul("nd,ne->de", context_tok, grad_attn)
        layer_grad_context = matmul("ne,de->nd", grad_attn, w_out).astype(jnp.bfloat16)
        grad_context_h = lax.all_to_all(
            split_heads(layer_grad_context, ROWS_MB, local),
            "seq",
            split_axis=0,
            concat_axis=1,
            tiled=True,
        )
        scores = masked_scores(query_h, keys_h, masking)
        prob_back = jnp.exp(scores - log_total)
        grad_prob = matmul("pqd,pkd->pqk", grad_context_h, values_h)
        inner_sum = jnp.sum(prob_back * grad_prob, -1, keepdims=True)
        grad_scores = (prob_back * (grad_prob - inner_sum)).astype(jnp.bfloat16)
        layer_grad_query = (matmul("pqk,pkd->pqd", grad_scores, keys_h) * scale).astype(
            jnp.bfloat16
        )
        layer_grad_keys = (matmul("pqk,pqd->pkd", grad_scores, query_h) * scale).astype(
            jnp.bfloat16
        )
        layer_grad_values = matmul(
            "pqk,pqd->pkd", prob_back.astype(jnp.bfloat16), grad_context_h
        ).astype(jnp.bfloat16)
        back_query, back_keys, back_values = heads_grads_out(
            layer_grad_query, layer_grad_keys, layer_grad_values
        )
        grad_w_query = matmul("nd,ne->de", inputs, back_query)
        grad_b_query = column_sum(back_query)
        grad_w_key = matmul("nd,ne->de", inputs, back_keys)
        grad_w_value = matmul("nd,ne->de", inputs, back_values)
        grad_b_value = column_sum(back_values)
        grad_input = (
            grad_resid_one
            + matmul("ne,de->nd", back_query, w_query)
            + matmul("ne,de->nd", back_keys, w_key)
            + matmul("ne,de->nd", back_values, w_value)
        )
        block_grads = (
            grad_w_query,
            grad_b_query,
            grad_w_key,
            grad_w_value,
            grad_b_value,
            grad_w_out,
            grad_b_out,
            grad_gain_one,
            grad_shift_one,
            grad_w_inner,
            grad_b_inner,
            grad_w_outer,
            grad_b_outer,
            grad_gain_two,
            grad_shift_two,
        )
        result, grad_input, block_grads = (
            result.astype(jnp.bfloat16),
            grad_input.astype(jnp.bfloat16),
            block_grads,
        )
        results.append(result.reshape(ROWS_MB, local, width))
        input_grads.append(grad_input.reshape(ROWS_MB, local, width))
        running = (
            block_grads
            if running is None
            else tuple((total + piece for total, piece in zip(running, block_grads)))
        )
    output = jnp.concatenate(results, 0)
    grad_tokens = jnp.concatenate(input_grads, 0)
    row_shares = jax.tree.map(
        lambda part: part.astype(jnp.float32),
        lax.psum_scatter(as_sent(running), "dp", scatter_dimension=0, tiled=True),
    )
    matrix_slots = (0, 2, 3, 5, 9, 11)
    vector_slots = (1, 4, 6, 7, 8, 10, 12, 13, 14)
    matrices = jax.tree.map(
        lambda part: part.astype(jnp.float32),
        lax.psum_scatter(
            as_sent(tuple((row_shares[slot] for slot in matrix_slots))),
            "seq",
            scatter_dimension=1,
            tiled=True,
        ),
    )
    vectors = lax.psum(tuple((row_shares[slot] for slot in vector_slots)), "seq")
    finished = [None] * 15
    for slot, piece in zip(matrix_slots, matrices):
        finished[slot] = piece
    for slot, piece in zip(vector_slots, vectors):
        finished[slot] = piece
    return (output, grad_tokens) + tuple(finished)


def solution(mesh):
    placed = (
        P("dp", "seq", None),
        P("dp", "seq", None),
        P("dp", "seq"),
        P(),
        P(),
        P(),
        P(),
        P(),
        P(),
        P(),
        P(),
        P(),
        P(),
        P(),
        P(),
        P(),
        P(),
        P(),
    )
    return jax.shard_map(
        body,
        mesh=mesh,
        in_specs=placed,
        out_specs=(
            P("dp", "seq", None),
            P("dp", "seq", None),
            P("dp", "seq"),
            P("dp"),
            P("dp", "seq"),
            P("dp", "seq"),
            P("dp"),
            P("dp", "seq"),
            P("dp"),
            P("dp"),
            P("dp"),
            P("dp", "seq"),
            P("dp"),
            P("dp", "seq"),
            P("dp"),
            P("dp"),
            P("dp"),
        ),
        check_vma=False,
    )
```

profile of v0, /device:TPU:0, one launch (start us, length us, event | category | flops | bytes accessed | tf_op | source)
XLA Modules:
  0.0 1028.9 jit_solution(6029302571591671209)
XLA Ops:
  41.3 6.1 all_gather.3
  82.5 6.0 all-to-all-done.12
  92.0 5.6 fusion.303
  114.6 4.8 fusion.87
  125.6 4.9 fusion.306
  148.0 4.8 fusion.89
  158.9 4.9 fusion.309
  192.3 4.8 fusion.88
  208.7 4.8 fusion.90
  261.6 5.9 multiply_convert_fusion.6
  284.0 5.8 multiply_convert_fusion.7
  359.6 4.6 add_convert_fusion.2
  383.8 7.2 multiply_reduce_fusion.1
  391.0 6.4 multiply_convert_fusion.1
  415.4 4.4 multiply_reduce_fusion.3
  571.0 6.8 fusion.273
  603.7 6.6 fusion.283
  610.3 5.1 fusion.278
  615.4 10.7 %add_convert_fusion = bf16[3072,768]{1,0:T(8,128)(2,1)} fusion(f32[3072,768]{1,0:T(8,128)S(1)} %bitcast.707, f32[3072,768]{1,0:T(8,128)} %fusion.283, f32[3072,768]{1,0:T(8,128)} %fusion.278, f32[256,768]{1,0:T(8,128)S(1)} %copy-done.83, f32[256,3072]{1,0:T(8,128)} %copy-done.80), kind=kOutput, calls=%fused_computation.4 | convolution fusion | flops 1221525504 | bytes 36962304 | tf_op jit(solution)/shard_map/nf,nd->fd/dot_general | solution.py:43
  630.5 5.3 fusion.294
  635.8 5.1 fusion.291
  641.0 10.7 %add_convert_fusion.1 = bf16[768,3072]{1,0:T(8,128)(2,1)} fusion(f32[768,3072]{1,0:T(8,128)S(1)} %fusion.288, f32[768,3072]{1,0:T(8,128)} %fusion.294, f32[768,3072]{1,0:T(8,128)} %fusion.291, bf16[256,3072]{1,0:T(8,128)(2,1)} %copy-done.91, f32[256,768]{1,0:T(8,128)S(1)} %copy-done.36, f32[256]{0:T(256)S(1)} %copy-done.184, f32[256]{0:T(256)S(1)} %copy-done.156, ...), kind=kOutput, calls=%fused_computation.5 | convolution fusion | flops 1218379776 | bytes 35397632 | tf_op jit(solution)/shard_map/nd,nf->df/dot_general | solution.py:43
  669.5 40.0 %all-reduce.10 = (bf16[768]{0:T(1024)(128)(2,1)S(1)}, bf16[768]{0:T(1024)(128)(2,1)S(1)}, bf16[768]{0:T(1024)(128)(2,1)S(1)}, bf16[768]{0:T(1024)(128)(2,1)S(1)}...) all-reduce(bf16[768]{0:T(1024)(128)(2,1)S(1)} %convert_element_type, ...), channel_id=4, replica_groups=mesh['dp'=8,'seq'=4] {'dp'}, use_global_device_ids=true, to_apply=%region_50.52.clone | all-reduce | flops 9216 | bytes 36864
  733.1 49.7 %reduce-scatter.35.cloned.1.call-done = bf16[384,768]{1,0:T(8,128)(2,1)} async-done(((bf16[3072,768]{1,0:T(8,128)(2,1)}), bf16[384,768]{1,0:T(8,128)(2,1)}) %reduce-scatter.35.cloned.1.call-update) | async-done | bytes 589840 | tf_op jit(solution)/shard_map/reduce_scatter | solution.py:265
  791.0 90.3 %reduce-scatter.31.cloned.1.call-done = bf16[96,3072]{1,0:T(8,128)(2,1)} async-done(((bf16[768,3072]{1,0:T(8,128)(2,1)}), bf16[96,3072]{1,0:T(8,128)(2,1)}) %reduce-scatter.31.cloned.1.call-update) | async-done | bytes 589840 | tf_op jit(solution)/shard_map/reduce_scatter | solution.py:265
  883.4 7.6 all-reduce.9
  895.5 7.8 reduce-scatter.43.cloned.1.call-done
  904.9 21.2 %reduce-scatter.23.cloned.1.call-done = bf16[96,192]{0,1:T(8,128)(2,1)} async-done(((bf16[96,768]{0,1:T(8,128)(2,1)}), bf16[96,192]{0,1:T(8,128)(2,1)}) %reduce-scatter.23.cloned.1.call-update) | async-done | bytes 36880 | tf_op jit(solution)/shard_map/reduce_scatter | solution.py:271
  927.6 21.2 %reduce-scatter.25.cloned.1.call-done = bf16[96,192]{0,1:T(8,128)(2,1)} async-done(((bf16[96,768]{0,1:T(8,128)(2,1)}), bf16[96,192]{0,1:T(8,128)(2,1)}) %reduce-scatter.25.cloned.1.call-update) | async-done | bytes 36880 | tf_op jit(solution)/shard_map/reduce_scatter | solution.py:271
  950.4 20.5 %reduce-scatter.27.cloned.1.call-done = bf16[96,192]{0,1:T(8,128)(2,1)} async-done(((bf16[96,768]{0,1:T(8,128)(2,1)}), bf16[96,192]{0,1:T(8,128)(2,1)}) %reduce-scatter.27.cloned.1.call-update) | async-done | bytes 36880 | tf_op jit(solution)/shard_map/reduce_scatter | solution.py:271
  972.4 23.1 %reduce-scatter.45.cloned.1.call-done = bf16[192,384]{1,0:T(8,128)(2,1)} async-done(((bf16[768,384]{1,0:T(8,128)(2,1)}), bf16[192,384]{1,0:T(8,128)(2,1)}) %reduce-scatter.45.cloned.1.call-update) | async-done | bytes 147472
  997.4 22.6 %reduce-scatter.33.cloned.1.call-done = bf16[96,768]{1,0:T(8,128)(2,1)} async-done(((bf16[96,3072]{1,0:T(8,128)(2,1)}), bf16[96,768]{1,0:T(8,128)(2,1)}) %reduce-scatter.33.cloned.1.call-update) | async-done | bytes 147472 | tf_op jit(solution)/shard_map/reduce_scatter | solution.py:271
  (911 shorter events, 573.8 us)
Async XLA Ops:
  17.3 60.2 %all-to-all-start.13 = ((bf16[24,128,64]{1,2,0:T(8,128)(2,1)}), bf16[24,128,64]{1,2,0:T(8,128)(2,1)}, u32[]{:S(2)}, u32[]{:S(2)}) async-start(bf16[24,128,64]{1,2,0:T(8,128)(2,1)} %bitcast.836), calls=%async_computation.13 | async-start | bytes 786432 | tf_op jit(solution)/shard_map/all_to_all | solution.py:137
  110.5 11.6 %all-to-all-start.4 = ((bf16[24,128,64]{1,2,0:T(8,128)(2,1)}), bf16[24,128,64]{1,2,0:T(8,128)(2,1)}, u32[]{:S(2)}, u32[]{:S(2)}) async-start(bf16[24,128,64]{1,2,0:T(8,128)(2,1)} %bitcast.20), calls=%async_computation.4 | async-start | bytes 786432 | tf_op jit(solution)/shard_map/all_to_all | solution.py:130
  143.8 11.6 %all-to-all-start = ((bf16[24,128,64]{1,2,0:T(8,128)(2,1)}), bf16[24,128,64]{1,2,0:T(8,128)(2,1)}, u32[]{:S(2)}, u32[]{:S(2)}) async-start(bf16[24,128,64]{1,2,0:T(8,128)(2,1)} %bitcast.2), calls=%async_computation | async-start | bytes 786432 | tf_op jit(solution)/shard_map/all_to_all | solution.py:130
  188.8 15.9 %all-to-all-start.2 = ((bf16[24,128,64]{1,2,0:T(8,128)(2,1)}), bf16[24,128,64]{1,2,0:T(8,128)(2,1)S(1)}, u32[]{:S(2)}, u32[]{:S(2)}) async-start(bf16[24,128,64]{1,2,0:T(8,128)(2,1)} %bitcast.833), calls=%async_computation.2 | async-start | bytes 786432 | tf_op jit(solution)/shard_map/all_to_all | solution.py:144
  204.7 26.7 %all-to-all-start.15 = ((bf16[4,2,24576]{2,1,0:T(2,128)(2,1)}), bf16[4,2,24576]{2,1,0:T(2,128)(2,1)S(1)}, u32[]{:S(2)}, u32[]{:S(2)}) async-start(bf16[4,2,24576]{2,1,0:T(2,128)(2,1)} %reshape.721), calls=%async_computation.15 | async-start | bytes 786432 | tf_op jit(solution)/shard_map/all_to_all | solution.py:161
  231.4 17.3 %all-to-all-start.7 = ((bf16[4,2,24576]{2,1,0:T(2,128)(2,1)}), bf16[4,2,24576]{2,1,0:T(2,128)(2,1)}, u32[]{:S(2)}, u32[]{:S(2)}) async-start(bf16[4,2,24576]{2,1,0:T(2,128)(2,1)} %reshape.723), calls=%async_computation.7 | async-start | bytes 786432 | tf_op jit(solution)/shard_map/all_to_all | solution.py:161
  248.6 22.2 %all-to-all-start.3 = ((bf16[4,2,24576]{2,1,0:T(2,128)(2,1)}), bf16[4,2,24576]{2,1,0:T(2,128)(2,1)}, u32[]{:S(2)}, u32[]{:S(2)}) async-start(bf16[4,2,24576]{2,1,0:T(2,128)(2,1)} %reshape.719), calls=%async_computation.3 | async-start | bytes 786432 | tf_op jit(solution)/shard_map/all_to_all | solution.py:161
  270.8 22.3 %all-to-all-start.11 = ((bf16[4,2,24576]{2,1,0:T(2,128)(2,1)}), bf16[4,2,24576]{2,1,0:T(2,128)(2,1)}, u32[]{:S(2)}, u32[]{:S(2)}) async-start(bf16[4,2,24576]{2,1,0:T(2,128)(2,1)} %reshape.715), calls=%async_computation.11 | async-start | bytes 786432 | tf_op jit(solution)/shard_map/all_to_all | solution.py:161
  350.0 14.3 %all-to-all-start.28 = ((bf16[24,128,64]{1,2,0:T(8,128)(2,1)}), bf16[24,128,64]{1,2,0:T(8,128)(2,1)S(1)}, u32[]{:S(2)}, u32[]{:S(2)}) async-start(bf16[24,128,64]{1,2,0:T(8,128)(2,1)} %bitcast.132), calls=%async_computation.28 | async-start | bytes 786432 | tf_op jit(solution)/shard_map/all_to_all | solution.py:197
  353.5 360.6 %reduce-scatter.29.cloned.1.call-start = ((), (), s32[]{:S(2)}) async-start(), calls=%async_computation.47 | async-start | bytes 1327104 | tf_op jit(solution)/shard_map/reduce_scatter | solution.py:265
  364.3 15.7 %all-to-all-start.24 = ((bf16[24,128,64]{1,2,0:T(8,128)(2,1)}), bf16[24,128,64]{1,2,0:T(8,128)(2,1)S(1)}, u32[]{:S(2)}, u32[]{:S(2)}) async-start(bf16[24,128,64]{1,2,0:T(8,128)(2,1)} %bitcast.113), calls=%async_computation.24 | async-start | bytes 786432 | tf_op jit(solution)/shard_map/all_to_all | solution.py:197
  380.0 18.5 %all-to-all-start.20 = ((bf16[24,128,64]{1,2,0:T(8,128)(2,1)}), bf16[24,128,64]{1,2,0:T(8,128)(2,1)S(1)}, u32[]{:S(2)}, u32[]{:S(2)}) async-start(bf16[24,128,64]{1,2,0:T(8,128)(2,1)} %bitcast.94), calls=%async_computation.20 | async-start | bytes 786432 | tf_op jit(solution)/shard_map/all_to_all | solution.py:197
  398.6 12.9 %all-to-all-start.16 = ((bf16[24,128,64]{1,2,0:T(8,128)(2,1)}), bf16[24,128,64]{1,2,0:T(8,128)(2,1)S(1)}, u32[]{:S(2)}, u32[]{:S(2)}) async-start(bf16[24,128,64]{1,2,0:T(8,128)(2,1)} %bitcast.75), calls=%async_computation.16 | async-start | bytes 786432 | tf_op jit(solution)/shard_map/all_to_all | solution.py:197
  411.5 20.5 %all-to-all-start.29 = ((bf16[4,2,24576]{2,1,0:T(2,128)(2,1)}), bf16[4,2,24576]{2,1,0:T(2,128)(2,1)S(1)}, u32[]{:S(2)}, u32[]{:S(2)}) async-start(bf16[4,2,24576]{2,1,0:T(2,128)(2,1)} %reshape.729), calls=%async_computation.29 | async-start | bytes 786432 | tf_op jit(solution)/shard_map/all_to_all | solution.py:105
  454.5 19.1 %all-to-all-start.17 = ((bf16[4,2,24576]{2,1,0:T(2,128)(2,1)}), bf16[4,2,24576]{2,1,0:T(2,128)(2,1)S(1)}, u32[]{:S(2)}, u32[]{:S(2)}) async-start(bf16[4,2,24576]{2,1,0:T(2,128)(2,1)} %reshape.725), calls=%async_computation.17 | async-start | bytes 786432 | tf_op jit(solution)/shard_map/all_to_all | solution.py:105
  473.6 12.5 %all-to-all-start.30 = ((bf16[4,2,24576]{2,1,0:T(2,128)(2,1)}), bf16[4,2,24576]{2,1,0:T(2,128)(2,1)}, u32[]{:S(2)}, u32[]{:S(2)}) async-start(bf16[4,2,24576]{2,1,0:T(2,128)(2,1)} %reshape.737), calls=%async_computation.30 | async-start | bytes 786432 | tf_op jit(solution)/shard_map/all_to_all | solution.py:106
  477.7 240.7 %reduce-scatter.37.cloned.1.call-start = ((), (), s32[]{:S(2)}) async-start(), calls=%async_computation.51 | async-start | bytes 1327104
  509.5 19.8 %all-to-all-start.18 = ((bf16[4,2,24576]{2,1,0:T(2,128)(2,1)}), bf16[4,2,24576]{2,1,0:T(2,128)(2,1)}, u32[]{:S(2)}, u32[]{:S(2)}) async-start(bf16[4,2,24576]{2,1,0:T(2,128)(2,1)} %reshape.733), calls=%async_computation.18 | async-start | bytes 786432 | tf_op jit(solution)/shard_map/all_to_all | solution.py:106
  529.3 14.3 %all-to-all-start.31 = ((bf16[4,2,24576]{2,1,0:T(2,128)(2,1)}), bf16[4,2,24576]{2,1,0:T(2,128)(2,1)}, u32[]{:S(2)}, u32[]{:S(2)}) async-start(bf16[4,2,24576]{2,1,0:T(2,128)(2,1)} %reshape.745), calls=%async_computation.31 | async-start | bytes 786432 | tf_op jit(solution)/shard_map/all_to_all | solution.py:107
  533.4 189.5 %reduce-scatter.39.cloned.1.call-start = ((), (), s32[]{:S(2)}) async-start(), calls=%async_computation.52 | async-start | bytes 1327104
  543.6 11.6 %all-to-all-start.27 = ((bf16[4,2,24576]{2,1,0:T(2,128)(2,1)}), bf16[4,2,24576]{2,1,0:T(2,128)(2,1)}, u32[]{:S(2)}, u32[]{:S(2)}) async-start(bf16[4,2,24576]{2,1,0:T(2,128)(2,1)} %reshape.739), calls=%async_computation.27 | async-start | bytes 786432 | tf_op jit(solution)/shard_map/all_to_all | solution.py:107
  555.2 11.6 %all-to-all-start.23 = ((bf16[4,2,24576]{2,1,0:T(2,128)(2,1)}), bf16[4,2,24576]{2,1,0:T(2,128)(2,1)}, u32[]{:S(2)}, u32[]{:S(2)}) async-start(bf16[4,2,24576]{2,1,0:T(2,128)(2,1)} %reshape.743), calls=%async_computation.23 | async-start | bytes 786432 | tf_op jit(solution)/shard_map/all_to_all | solution.py:107
  566.8 26.9 %all-to-all-start.19 = ((bf16[4,2,24576]{2,1,0:T(2,128)(2,1)}), bf16[4,2,24576]{2,1,0:T(2,128)(2,1)}, u32[]{:S(2)}, u32[]{:S(2)}) async-start(bf16[4,2,24576]{2,1,0:T(2,128)(2,1)} %reshape.741), calls=%async_computation.19 | async-start | bytes 786432 | tf_op jit(solution)/shard_map/all_to_all | solution.py:107
  570.9 156.5 %reduce-scatter.41.cloned.1.call-start = ((), (), s32[]{:S(2)}) async-start(), calls=%async_computation.53 | async-start | bytes 1327104
  603.4 179.4 %reduce-scatter.35.cloned.1.call-start = ((), (), s32[]{:S(2)}) async-start(), calls=%async_computation.50 | async-start | bytes 5308416 | tf_op jit(solution)/shard_map/reduce_scatter | solution.py:265
  626.2 255.2 %reduce-scatter.31.cloned.1.call-start = ((), (), s32[]{:S(2)}) async-start(), calls=%async_computation.48 | async-start | bytes 5308416 | tf_op jit(solution)/shard_map/reduce_scatter | solution.py:265
  651.8 251.5 %reduce-scatter.43.cloned.1.call-start = ((), (), s32[]{:S(2)}) async-start(), calls=%async_computation.54 | async-start | bytes 245760
  715.9 210.2 %reduce-scatter.23.cloned.1.call-start = ((), (), s32[]{:S(2)}) async-start(), calls=%async_computation.44 | async-start | bytes 245760 | tf_op jit(solution)/shard_map/reduce_scatter | solution.py:271
  720.1 228.7 %reduce-scatter.25.cloned.1.call-start = ((), (), s32[]{:S(2)}) async-start(), calls=%async_computation.45 | async-start | bytes 245760 | tf_op jit(solution)/shard_map/reduce_scatter | solution.py:271
  724.7 246.2 %reduce-scatter.27.cloned.1.call-start = ((), (), s32[]{:S(2)}) async-start(), calls=%async_computation.46 | async-start | bytes 245760 | tf_op jit(solution)/shard_map/reduce_scatter | solution.py:271
  729.2 266.3 %reduce-scatter.45.cloned.1.call-start = ((), (), s32[]{:S(2)}) async-start(), calls=%async_computation.55 | async-start | bytes 737280
  785.0 235.0 %reduce-scatter.33.cloned.1.call-start = ((), (), s32[]{:S(2)}) async-start(), calls=%async_computation.49 | async-start | bytes 737280 | tf_op jit(solution)/shard_map/reduce_scatter | solution.py:271
  (247 other events, 2262.8 us)
Sparse Core Ops, SparseCore 0:
  364.4 66.1 reduce-scatter.28
  486.2 66.1 reduce-scatter.36
  555.7 62.9 reduce-scatter.38
  622.0 63.0 reduce-scatter.40
  688.5 94.2 reduce-scatter.34
  786.3 94.9 reduce-scatter.30
  883.8 19.4 reduce-scatter.42
  906.3 19.7 reduce-scatter.22
  929.1 19.7 reduce-scatter.24
  951.1 19.7 reduce-scatter.26
  973.4 22.0 reduce-scatter.44
  997.8 22.0 reduce-scatter.32
where the time goes:
time: 1040 us; the launch traced here: 1030 us
  waiting for transfers between devices  291 us (28%)
  matrix products  261 us (25%)
  local copies, waits for them, and re-layouts  205 us (20%)
  starting transfers between devices  121 us (12%)
  other arithmetic  76.5 us (7%)
  blocking collectives  53.8 us (5%)
  between operations  19.6 us (2%)
    dot_general x72, matrix products, matmul(): return jnp.einsum(pattern, left, right, preferred_element_type=jnp.float32)  212 us
    reduce_scatter x3, waiting for transfers between devices, body(): lax.psum_scatter(as_sent(running), 'dp', scatter_dimension=0, tiled=True)  140 us
    unnamed x517, local copies, waits for them, and re-layouts  97.3 us
    reduce_scatter x4, waiting for transfers between devices, body(): lax.psum_scatter(as_sent(tuple((row_shares[slot] for slot in matrix_slots...  85.6 us
    unnamed x1, blocking collectives  40 us
    unnamed x17, waiting for transfers between devices  31.1 us
  transfers between devices with their start and end apart: 44, of which 24 were waited for; matrix products, arithmetic and copies ran while one was open for 45% of the time, Pallas kernels for 0%

commit v1 on v0

v1 whole, which is shorter than its diff:
```python
import jax
import jax.numpy as jnp
from jax import lax
from jax.sharding import PartitionSpec as P

HEADS = 12
BF = jnp.bfloat16
F32 = jnp.float32


def layer_norm(values, gain, shift):
    centred = values - jnp.mean(values, -1, keepdims=True)
    inverse = lax.rsqrt(jnp.mean(centred * centred, -1, keepdims=True) + 1e-05)
    normed = centred * inverse
    return (normed * gain.astype(F32) + shift.astype(F32), normed, inverse)


def norm_back(upstream, normed, inverse, gain):
    scaled = upstream * gain.astype(F32)
    return inverse * (
        scaled
        - jnp.mean(scaled, -1, keepdims=True)
        - normed * jnp.mean(scaled * normed, -1, keepdims=True)
    )


def matmul(pattern, left, right):
    return jnp.einsum(pattern, left, right, preferred_element_type=F32)


def column_sum(values):
    return jnp.sum(values.astype(F32), 0)


def swap(array, axis, mask):
    size = lax.axis_size(axis)
    return lax.ppermute(array, axis, [(i, i ^ mask) for i in range(size)])


def rows_in(array):
    n = lax.axis_size("seq")
    me = lax.axis_index("seq")
    rows = array.shape[0] // n
    blocks = []
    for k in range(n):
        block = lax.dynamic_slice_in_dim(array, (me ^ k) * rows, rows, 0)
        blocks.append(swap(block, "seq", k) if k else block)
    return jnp.concatenate(blocks, 1)


def rows_out(array):
    n = lax.axis_size("seq")
    me = lax.axis_index("seq")
    rows, length = array.shape[0], array.shape[1] // n
    whole = jnp.zeros((rows * n, length) + array.shape[2:], array.dtype)
    for k in range(n):
        block = lax.slice_in_dim(array, k * length, (k + 1) * length, axis=1)
        block = swap(block, "seq", k) if k else block
        whole = lax.dynamic_update_slice_in_dim(whole, block, (me ^ k) * rows, 0)
    return whole


def bits_of(size):
    return [1 << b for b in range(size.bit_length() - 1)]


def halving_order():
    seq_bits = [("seq", m) for m in bits_of(lax.axis_size("seq"))]
    dp_bits = [("dp", m) for m in bits_of(lax.axis_size("dp"))]
    return [seq_bits[0], dp_bits[0]] + seq_bits[1:] + dp_bits[1:]


def reduce_matrix(grad):
    sn, dn = lax.axis_size("seq"), lax.axis_size("dp")
    ms, md = lax.axis_index("seq"), lax.axis_index("dp")
    high, wide = grad.shape[0] // dn, grad.shape[1] // sn
    blocks = grad.astype(BF).reshape(dn, high, sn, wide).transpose(2, 0, 1, 3)
    blocks = jnp.take(blocks, ms ^ jnp.arange(sn), axis=0)
    blocks = jnp.take(blocks, md ^ jnp.arange(dn), axis=1)
    left = {"seq": sn, "dp": dn}
    for axis, mask in halving_order():
        size = left[axis]
        dim = 0 if axis == "seq" else 1
        shape = blocks.shape[:dim] + (size // 2, 2) + blocks.shape[dim + 1 :]
        split = blocks.reshape(shape)
        keep = lax.index_in_dim(split, 0, dim + 1, keepdims=False)
        send = lax.index_in_dim(split, 1, dim + 1, keepdims=False)
        blocks = keep + swap(send, axis, mask)
        left[axis] = size // 2
    return blocks.reshape(high, wide).astype(F32)


def reduce_vectors(vectors):
    scattered = lax.psum_scatter(tuple(vectors), "dp", scatter_dimension=0, tiled=True)
    return lax.psum(scattered, "seq")


def body(
    tokens,
    cotangent,
    segments,
    w_query,
    b_query,
    w_key,
    w_value,
    b_value,
    w_out,
    b_out,
    gain_one,
    shift_one,
    w_inner,
    b_inner,
    w_outer,
    b_outer,
    gain_two,
    shift_two,
):
    width = tokens.shape[-1]
    head_dim = width // HEADS
    scale = head_dim ** (-0.5)
    x_rows = rows_in(tokens)
    up_rows = rows_in(cotangent)
    seg_rows = rows_in(segments)
    rows, length = seg_rows.shape
    count = rows * length
    inputs = x_rows.reshape(count, width)
    upstream = up_rows.reshape(count, width).astype(F32)
    masking = (seg_rows[:, :, None] == seg_rows[:, None, :])[:, None]

    def split(values):
        return values.reshape(rows, length, HEADS, head_dim)

    query = (matmul("nd,de->ne", inputs, w_query) + b_query).astype(BF)
    keys = matmul("nd,de->ne", inputs, w_key).astype(BF)
    values = (matmul("nd,de->ne", inputs, w_value) + b_value).astype(BF)
    query_h, keys_h, values_h = split(query), split(keys), split(values)

    def masked_scores():
        raw = matmul("rqhd,rkhd->rhqk", query_h, keys_h) * scale
        return jnp.where(masking, raw, -1e30)

    scores = masked_scores()
    highest = jnp.max(scores, -1, keepdims=True)
    expo = jnp.exp(scores - highest)
    totals = jnp.sum(expo, -1, keepdims=True)
    prob = expo / totals
    log_total = highest + jnp.log(totals)
    context = matmul("rhqk,rkhd->rqhd", prob.astype(BF), values_h).astype(BF).reshape(count, width)
    resid_one = inputs.astype(F32) + matmul("nd,de->ne", context, w_out) + b_out
    hidden_one, normed_one, inverse_one = layer_norm(resid_one, gain_one, shift_one)
    hidden_low = hidden_one.astype(BF)
    inner = matmul("nd,df->nf", hidden_low, w_inner) + b_inner
    phi = 0.5 * (1.0 + lax.erf(inner * 0.7071067811865476))
    active = (inner * phi).astype(BF)
    resid_two = hidden_one + matmul("nf,fd->nd", active, w_outer) + b_outer
    result, normed_two, inverse_two = layer_norm(resid_two, gain_two, shift_two)
    output = rows_out(result.astype(BF).reshape(rows, length, width))
    grad_gain_two = jnp.sum(upstream * normed_two, 0)
    grad_shift_two = jnp.sum(upstream, 0)
    grad_resid_two = norm_back(upstream, normed_two, inverse_two, gain_two)
    grad_branch = grad_resid_two.astype(BF)
    grad_b_outer = column_sum(grad_branch)
    grad_w_outer = reduce_matrix(matmul("nf,nd->fd", active, grad_branch))
    slope = phi + inner * jnp.exp(-0.5 * inner * inner) * 0.3989422804014327
    grad_inner = (matmul("nd,fd->nf", grad_branch, w_outer) * slope).astype(BF)
    grad_b_inner = column_sum(grad_inner)
    grad_w_inner = reduce_matrix(matmul("nd,nf->df", hidden_low, grad_inner))
    grad_hidden = grad_resid_two + matmul("nf,df->nd", grad_inner, w_inner)
    grad_gain_one = jnp.sum(grad_hidden * normed_one, 0)
    grad_shift_one = jnp.sum(grad_hidden, 0)
    grad_resid_one = norm_back(grad_hidden, normed_one, inverse_one, gain_one)
    grad_attn = grad_resid_one.astype(BF)
    grad_b_out = column_sum(grad_attn)
    grad_w_out = reduce_matrix(matmul("nd,ne->de", context, grad_attn))
    grad_context = split(matmul("ne,de->nd", grad_attn, w_out).astype(BF))
    prob_back = jnp.exp(masked_scores() - log_total)
    grad_prob = matmul("rqhd,rkhd->rhqk", grad_context, values_h)
    inner_sum = jnp.sum(prob_back * grad_prob, -1, keepdims=True)
    grad_scores = (prob_back * (grad_prob - inner_sum)).astype(BF)
    grad_query = (matmul("rhqk,rkhd->rqhd", grad_scores, keys_h) * scale).astype(BF)
    grad_keys = (matmul("rhqk,rqhd->rkhd", grad_scores, query_h) * scale).astype(BF)
    grad_values = matmul("rhqk,rqhd->rkhd", prob_back.astype(BF), grad_context).astype(BF)
    grad_query, grad_keys, grad_values = (
        piece.reshape(count, width) for piece in (grad_query, grad_keys, grad_values)
    )
    grad_w_query = reduce_matrix(matmul("nd,ne->de", inputs, grad_query))
    grad_w_key = reduce_matrix(matmul("nd,ne->de", inputs, grad_keys))
    grad_w_value = reduce_matrix(matmul("nd,ne->de", inputs, grad_values))
    grad_b_query = column_sum(grad_query)
    grad_b_value = column_sum(grad_values)
    grad_input = (
        grad_resid_one
        + matmul("ne,de->nd", grad_query, w_query)
        + matmul("ne,de->nd", grad_keys, w_key)
        + matmul("ne,de->nd", grad_values, w_value)
    ).astype(BF)
    grad_tokens = rows_out(grad_input.reshape(rows, length, width))
    (
        grad_b_query,
        grad_b_value,
        grad_b_out,
        grad_gain_one,
        grad_shift_one,
        grad_b_inner,
        grad_b_outer,
        grad_gain_two,
        grad_shift_two,
    ) = reduce_vectors(
        (
            grad_b_query,
            grad_b_value,
            grad_b_out,
            grad_gain_one,
            grad_shift_one,
            grad_b_inner,
            grad_b_outer,
            grad_gain_two,
            grad_shift_two,
        )
    )
    return (
        output,
        grad_tokens,
        grad_w_query,
        grad_b_query,
        grad_w_key,
        grad_w_value,
        grad_b_value,
        grad_w_out,
        grad_b_out,
        grad_gain_one,
        grad_shift_one,
        grad_w_inner,
        grad_b_inner,
        grad_w_outer,
        grad_b_outer,
        grad_gain_two,
        grad_shift_two,
    )


def solution(mesh):
    token = P("dp", "seq", None)
    matrix = P("dp", "seq")
    vector = P("dp")
    return jax.shard_map(
        body,
        mesh=mesh,
        in_specs=(token, token, P("dp", "seq")) + (P(),) * 15,
        out_specs=(
            token,
            token,
            matrix,
            vector,
            matrix,
            matrix,
            vector,
            matrix,
            vector,
            vector,
            vector,
            matrix,
            vector,
            matrix,
            vector,
            vector,
            vector,
        ),
        check_vma=False,
    )
```

time: 1040 us -> 637 us (0.61)
  waiting for transfers between devices: 291 us -> 124 us
  matrix products: 261 us -> 157 us
  starting transfers between devices: 121 us -> 34.7 us
  between operations: 19.6 us -> 3.64 us
  local copies, waits for them, and re-layouts: 205 us -> 190 us
    reduce_scatter x7 -> x0, waiting for transfers between devices: 226 us -> none  [the longest x3 140 us: body(): lax.psum_scatter(as_sent(running), 'dp', scatter_dimension=0, tiled=True)]
    ppermute x0 -> x45, waiting for transfers between devices: none -> 124 us  [swap(): return lax.ppermute(array, axis, [(i, i ^ mask) for i in range(size)])]
    all_to_all x32 -> x0, starting transfers between devices: 121 us -> none  [the longest x4 16.5 us: heads_grads_out(): lax.all_to_all(grad_values, 'seq', split_axis=1, concat_axis=0, tiled=True)]
    dot_general x96 -> x24, matrix products: 261 us -> 157 us  [matmul(): return jnp.einsum(pattern, left, right, preferred_element_type=F32)]
    reshape x16, local copies, waits for them, and re-layouts: 4.02 us -> 73.7 us  [the longest x12 60.7 us: reduce_matrix(): blocks = grad.astype(BF).reshape(dn, high, sn, wide).transpose(2, 0, 1, 3)]
    unnamed x517 -> x139, local copies, waits for them, and re-layouts: 97.3 us -> 31.1 us
    gather x4 -> x13, local copies, waits for them, and re-layouts: 4.63 us -> 49.1 us  [the longest x7 26 us: reduce_matrix(): blocks = jnp.take(blocks, md ^ jnp.arange(dn), axis=1)]
    all_to_all x32 -> x0, waiting for transfers between devices: 34.7 us -> none  [the longest x4 14.6 us: body(): lax.all_to_all(split_heads(projections_query, ROWS_MB, local), 'seq', spl...]
  transfers between devices with their start and end apart: 44 -> 45, of which waited for: 24 -> 17; matrix products, arithmetic and copies ran while one was open for 45% -> 19% of each run, Pallas kernels for 0% -> 0%
where the time goes in v1:
time: 637 us; the launch traced here: 631 us
  local copies, waits for them, and re-layouts  190 us (30%)
  matrix products  157 us (25%)
  waiting for transfers between devices  124 us (19%)
  other arithmetic  75.6 us (12%)
  blocking collectives  45.8 us (7%)
  starting transfers between devices  34.7 us (5%)
    dot_general x24, matrix products, matmul(): return jnp.einsum(pattern, left, right, preferred_element_type=F32)  157 us
    ppermute x45, waiting for transfers between devices, swap(): return lax.ppermute(array, axis, [(i, i ^ mask) for i in range(size)])  124 us
    reshape x12, local copies, waits for them, and re-layouts, reduce_matrix(): blocks = grad.astype(BF).reshape(dn, high, sn, wide).transpose(2, 0, 1, 3)  60.7 us
    unnamed x1, blocking collectives  39.1 us
    ppermute x45, starting transfers between devices, swap(): return lax.ppermute(array, axis, [(i, i ^ mask) for i in range(size)])  34.7 us
    unnamed x139, local copies, waits for them, and re-layouts  31.1 us
    gather x7, local copies, waits for them, and re-layouts, reduce_matrix(): blocks = jnp.take(blocks, md ^ jnp.arange(dn), axis=1)  26 us
    gather x6, local copies, waits for them, and re-layouts, reduce_matrix(): blocks = jnp.take(blocks, ms ^ jnp.arange(sn), axis=0)  23.2 us
  transfers between devices with their start and end apart: 45, of which 17 were waited for; matrix products, arithmetic and copies ran while one was open for 19% of the time, Pallas kernels for 0%

profile of v1, /device:TPU:0, one launch (start us, length us, event | category | flops | bytes accessed | tf_op | source)
XLA Modules:
  0.0 630.6 jit_solution(2706567943768887569)
XLA Ops:
  15.5 9.4 %collective-permute-done.4 = s32[2,128]{1,0:T(2,128)S(1)} collective-permute-done((s32[2,128]{1,0:T(2,128)S(1)}, s32[2,128]{1,0:T(2,128)S(1)}, u32[]{:S(2)}, u32[]{:S(2)}) %collective-permute-start.4) | collective-permute-done | bytes 1056 | tf_op jit(solution)/shard_map/ppermute | solution.py:37
  55.9 12.1 %fusion.12 = (f32[2,12,512]{2,1,0:T(8,128)S(1)}, f32[2,12,512,512]{2,3,1,0:T(8,128)}) fusion(pred[2,512,512]{1,2,0:T(8,128)(4,1)S(1)} %broadcast_compare_fusion, bf16[2,512,12,64]{1,0,3,2:T(2,128)(2,1)S(1)} %reshape.324, bf16[2,512,12,64]{1,0,3,2:T(2,128)(2,1)} %reshape.323), kind=kOutput, calls=%fused_computation.33 | convolution fusion | flops 824168448 | bytes 28884992 | tf_op jit(solution)/shard_map/rqhd,rkhd->rhqk/dot_general | solution.py:28
  68.0 11.1 %fusion = f32[2,12,512]{2,1,0:T(8,128)S(1)} fusion(f32[2,12,512]{2,1,0:T(8,128)S(1)} %get-tuple-element.88, f32[2,12,512,512]{2,3,1,0:T(8,128)} %get-tuple-element.89, pred[2,512,512]{1,2,0:T(8,128)(4,1)S(1)} %broadcast_compare_fusion), kind=kLoop, calls=%fused_computation.18 | loop fusion | flops 25153536 | bytes 25788416 | tf_op jit(solution)/shard_map/reduce_sum | solution.py:145
  79.1 12.0 %fusion.32 = bf16[2,512,12,64]{1,3,2,0:T(8,128)(2,1)S(1)} fusion(f32[2,12,512]{2,1,0:T(8,128)S(1)} %fusion, f32[2,12,512]{2,1,0:T(8,128)S(1)} %get-tuple-element.88, f32[2,12,512,512]{2,3,1,0:T(8,128)} %get-tuple-element.89, pred[2,512,512]{1,2,0:T(8,128)(4,1)S(1)} %broadcast_compare_fusion, bf16[2,512,12,64]{1,0,3,2:T(2,128)(2,1)S(1)} %copy-done.11), kind=kOutput, calls=%fused_computation.106 | convolution fusion | flops 837550080 | bytes 28934144 | tf_op jit(solution)/shard_map/rhqk,rkhd->rqhd/dot_general | solution.py:28
  96.1 9.1 %multiply_convert_fusion.1 = (bf16[1024,3072]{1,0:T(8,128)(2,1)S(1)}, f32[1024,3072]{1,0:T(8,128)}) fusion(f32[3072]{0:T(1024)S(1)} %convert_element_type.192, bf16[768,3072]{1,0:T(8,128)(2,1)S(1)} %bitcast.531, f32[1024,768]{1,0:T(8,128)S(1)} %get-tuple-element.50, f32[768]{0:T(1024)S(1)} %convert_element_type.190, f32[768]{0:T(1024)S(1)} %convert_element_type.189, ...), kind=kOutput, calls=%fused_computation.30 | convolution fusion | flops 4854644736 | bytes 26765312 | tf_op jit(solution)/shard_map/nd,df->nf/dot_general | solution.py:28
  105.2 5.4 fusion.116
  121.9 9.8 %convolution_convert_fusion = bf16[3072,768]{1,0:T(8,128)(2,1)} fusion(bf16[1024,3072]{1,0:T(8,128)(2,1)} %copy-done.51, f32[1024,768]{1,0:T(8,128)S(1)} %get-tuple-element.46), kind=kOutput, calls=%fused_computation.34 | convolution fusion | flops 4834983936 | bytes 14155776 | tf_op jit(solution)/shard_map/nf,nd->fd/dot_general | solution.py:28
  131.8 13.7 %convert_reduce_fusion = (f32[3072]{0:T(1024)}, bf16[1024,3072]{1,0:T(8,128)(2,1)}) fusion(f32[1024,3072]{1,0:T(8,128)} %get-tuple-element.91, f32[3072]{0:T(1024)S(1)} %convert_element_type.192, bf16[3072,768]{1,0:T(8,128)(2,1)S(1)} %bitcast.529, f32[1024,768]{1,0:T(8,128)S(1)} %get-tuple-element.46), kind=kOutput, calls=%fused_computation.28 | convolution fusion | flops 4873516032 | bytes 26763264 | tf_op jit(solution)/shard_map/nd,fd->nf/dot_general | solution.py:28
  145.5 9.9 %convolution_convert_fusion.1 = bf16[768,3072]{1,0:T(8,128)(2,1)} fusion(bf16[1024,3072]{1,0:T(8,128)(2,1)} %get-tuple-element.102, f32[1024,768]{1,0:T(8,128)S(1)} %get-tuple-element.50, f32[768]{0:T(1024)S(1)} %convert_element_type.190, f32[768]{0:T(1024)S(1)} %convert_element_type.189, f32[1024]{0:T(1024)S(1)} %add_rsqrt_fusion.1, ...), kind=kOutput, calls=%fused_computation.35 | convolution fusion | flops 4838129664 | bytes 14170112 | tf_op jit(solution)/shard_map/nd,nf->df/dot_general | solution.py:28
  155.3 8.8 %multiply_reduce_fusion.1 = (f32[768]{0:T(1024)}, f32[1024]{0:T(1024)S(1)}, f32[1024]{0:T(1024)S(1)}, f32[768]{0:T(1024)}, f32[1024,768]{1,0:T(8,128)S(1)}) fusion(f32[1024,768]{1,0:T(8,128)S(1)} %get-tuple-element.50, f32[1024]{0:T(1024)S(1)} %add_rsqrt_fusion.1, f32[1024]{0:T(1024)S(1)} %broadcast_multiply_fusion.4, f32[768]{0:T(1024)S(1)} %convert_element_type.189, ...), kind=kOutput, calls=%fused_computation.53 | convolution fusion | flops 4839698432 | bytes 20472832 | tf_op jit(solution)/shard_map/nf,df->nd/dot_general | solution.py:28
  176.6 13.4 %convert_reduce_fusion.4 = (f32[12,64]{1,0:T(8,128)}, bf16[2,512,12,64]{1,3,2,0:T(8,128)(2,1)}) fusion(f32[2,12,512]{2,1,0:T(8,128)S(1)} %log_add_fusion, f32[2,12,512,512]{2,3,1,0:T(8,128)} %get-tuple-element.89, pred[2,512,512]{1,2,0:T(8,128)(4,1)S(1)} %broadcast_compare_fusion, bf16[2,512,12,64]{1,0,3,2:T(2,128)(2,1)} %reshape.327), kind=kOutput, calls=%fused_computation.55 | convolution fusion | flops 832830720 | bytes 28888064 | tf_op jit(solution)/shard_map/rhqk,rqhd->rkhd/dot_general | solution.py:28
  190.0 18.1 %multiply_reduce_fusion = (f32[2,12,512]{2,1,0:T(8,128)S(1)}, f32[2,12,512,512]{2,3,1,0:T(8,128)}) fusion(f32[2,12,512]{2,1,0:T(8,128)S(1)} %log_add_fusion, f32[2,12,512,512]{2,3,1,0:T(8,128)} %get-tuple-element.89, pred[2,512,512]{1,2,0:T(8,128)(4,1)S(1)} %broadcast_compare_fusion, bf16[2,512,12,64]{1,0,3,2:T(2,128)(2,1)S(1)} %copy-done.11, ...), kind=kOutput, calls=%fused_computation.13 | convolution fusion | flops 836751360 | bytes 54099968 | tf_op jit(solution)/shard_map/rqhd,rkhd->rhqk/dot_general | solution.py:28
  208.1 17.4 %multiply_convert_fusion = bf16[2,12,512,512]{2,3,1,0:T(8,128)(2,1)S(1)} fusion(f32[2,12,512,512]{2,3,1,0:T(8,128)} %get-tuple-element.96, f32[2,12,512]{2,1,0:T(8,128)S(1)} %get-tuple-element.95, f32[2,12,512]{2,1,0:T(8,128)S(1)} %log_add_fusion, f32[2,12,512,512]{2,3,1,0:T(8,128)} %get-tuple-element.89, pred[2,512,512]{1,2,0:T(8,128)(4,1)S(1)} %broadcast_compare_fusion), kind=kLoop, calls=%fused_computation.12 | loop fusion | flops 37748736 | bytes 63537152 | tf_op jit(solution)/shard_map/convert_element_type | solution.py:179
  232.4 8.6 %fusion.31 = bf16[2,512,12,64]{1,3,2,0:T(8,128)(2,1)S(1)} fusion(bf16[2,12,512,512]{2,3,1,0:T(8,128)(2,1)} %copy-done.2, bf16[2,512,12,64]{1,0,3,2:T(2,128)(2,1)S(1)} %copy-done.7), kind=kOutput, calls=%fused_computation.105 | convolution fusion | flops 806879232 | bytes 15728640 | tf_op jit(solution)/shard_map/rhqk,rqhd->rkhd/dot_general | solution.py:28
  259.7 12.9 %reshape.493 = bf16[8,384,4,192]{3,2,1,0:T(4,128)(2,1)} reshape(bf16[3072,768]{1,0:T(8,128)(2,1)} %convolution_convert_fusion) | data formatting | bytes 9437184 | tf_op jit(solution)/shard_map/reshape | solution.py:77
  272.6 10.3 %copy.170 = bf16[8,384,4,192]{1,3,0,2:T(8,128)(2,1)} copy(bf16[8,384,4,192]{3,2,1,0:T(4,128)(2,1)} %reshape.493) | data formatting | bytes 9437184 | tf_op jit(solution)/shard_map/reshape | solution.py:77
  282.9 5.9 gather_fusion.2
  293.8 5.8 gather_fusion.3
  306.9 9.9 %reshape.356 = bf16[8,96,4,768]{3,2,1,0:T(4,128)(2,1)} reshape(bf16[768,3072]{1,0:T(8,128)(2,1)} %convolution_convert_fusion.1) | data formatting | bytes 9437184 | tf_op jit(solution)/shard_map/reshape | solution.py:77
  322.2 5.5 gather_fusion
  332.8 5.5 gather_fusion.1
  419.6 39.1 %all-reduce.9 = (f32[768]{0:T(1024)}, f32[768]{0:T(1024)}, f32[768]{0:T(1024)}, f32[768]{0:T(1024)}, f32[768]{0:T(1024)S(1)}, /*index=5*/f32[3072]{0:T(1024)}, f32[768]{0:T(1024)}, f32[768]{0:T(1024)}, f32[768]{0:T(1024)}) all-reduce(f32[768]{0:T(1024)} %reduce_sum.186, ...), channel_id=2, replica_groups=mesh['dp'=8,'seq'=4] {'dp'}, use_global_device_ids=true, to_apply=%region_12.15.clone | all-reduce | flops 9216 | bytes 73728
  468.4 6.7 %all-reduce.10 = (f32[96]{0:T(128)}, f32[96]{0:T(128)}, f32[96]{0:T(128)}, f32[96]{0:T(128)}, f32[96]{0:T(128)}, /*index=5*/f32[384]{0:T(512)}, f32[96]{0:T(128)}, f32[96]{0:T(128)}, f32[96]{0:T(128)}) all-reduce(f32[96]{0:T(128)S(1)} %dynamic-slice.1, f32[96]{0:T(128)} %dynamic-slice.3, ...), channel_id=1, replica_groups=mesh['dp'=8,'seq'=4] {'seq'}, use_global_device_ids=true, to_apply=%region_13.16 | all-reduce | flops 1152 | bytes 9216 | tf_op jit(solution)/shard_map/psum | solution.py:95
  488.1 5.6 collective-permute-done.8
  499.1 9.3 %collective-permute-done.31 = bf16[2,4,96,192]{3,2,1,0:T(8,128)(2,1)S(1)} collective-permute-done((bf16[2,4,96,192]{3,2,1,0:T(8,128)(2,1)S(1)}, bf16[2,4,96,192]{3,2,1,0:T(8,128)(2,1)S(1)}, u32[]{:S(2)}, u32[]{:S(2)}) %collective-permute-start.31) | collective-permute-done | bytes 294944 | tf_op jit(solution)/shard_map/ppermute | solution.py:37
  508.6 8.3 %collective-permute-done.26 = bf16[2,4,96,192]{3,2,1,0:T(8,128)(2,1)S(1)} collective-permute-done((bf16[2,4,96,192]{3,2,1,0:T(8,128)(2,1)S(1)}, bf16[2,4,96,192]{3,2,1,0:T(8,128)(2,1)S(1)}, u32[]{:S(2)}, u32[]{:S(2)}) %collective-permute-start.26) | collective-permute-done | bytes 294944 | tf_op jit(solution)/shard_map/ppermute | solution.py:37
  518.5 6.8 %collective-permute-done.21 = bf16[2,4,96,192]{3,2,1,0:T(8,128)(2,1)S(1)} collective-permute-done((bf16[2,4,96,192]{3,2,1,0:T(8,128)(2,1)S(1)}, bf16[2,4,96,192]{3,2,1,0:T(8,128)(2,1)S(1)}, u32[]{:S(2)}, u32[]{:S(2)}) %collective-permute-start.21) | collective-permute-done | bytes 294944 | tf_op jit(solution)/shard_map/ppermute | solution.py:37
  526.9 6.4 %collective-permute-done.16 = bf16[2,4,96,192]{3,2,1,0:T(8,128)(2,1)S(1)} collective-permute-done((bf16[2,4,96,192]{3,2,1,0:T(8,128)(2,1)S(1)}, bf16[2,4,96,192]{3,2,1,0:T(8,128)(2,1)S(1)}, u32[]{:S(2)}, u32[]{:S(2)}) %collective-permute-start.16) | collective-permute-done | bytes 294944 | tf_op jit(solution)/shard_map/ppermute | solution.py:37
  558.6 24.5 %collective-permute-done.41 = bf16[2,4,384,192]{2,3,1,0:T(8,128)(2,1)S(1)} collective-permute-done((bf16[2,4,384,192]{2,3,1,0:T(8,128)(2,1)S(1)}, bf16[2,4,384,192]{2,3,1,0:T(8,128)(2,1)S(1)}, u32[]{:S(2)}, u32[]{:S(2)}) %collective-permute-start.41) | collective-permute-done | bytes 1179680 | tf_op jit(solution)/shard_map/ppermute | solution.py:37
  585.0 19.3 %collective-permute-done.36 = bf16[2,4,96,768]{3,2,1,0:T(8,128)(2,1)S(1)} collective-permute-done((bf16[2,4,96,768]{3,2,1,0:T(8,128)(2,1)S(1)}, bf16[2,4,96,768]{3,2,1,0:T(8,128)(2,1)S(1)}, u32[]{:S(2)}, u32[]{:S(2)}) %collective-permute-start.36) | collective-permute-done | bytes 1179680 | tf_op jit(solution)/shard_map/ppermute | solution.py:37
  608.0 7.6 %collective-permute-done.37 = bf16[1,4,96,768]{3,2,1,0:T(8,128)(2,1)S(1)} collective-permute-done((bf16[1,4,96,768]{3,2,1,0:T(8,128)(2,1)S(1)}, bf16[1,4,96,768]{3,2,1,0:T(8,128)(2,1)S(1)}, u32[]{:S(2)}, u32[]{:S(2)}) %collective-permute-start.37) | collective-permute-done | bytes 589856 | tf_op jit(solution)/shard_map/ppermute | solution.py:37
  617.5 6.0 collective-permute-done.38
  (383 shorter events, 272.5 us)
Async XLA Ops:
  3.5 23.5 %collective-permute-start = (bf16[2,128,768]{2,1,0:T(8,128)(2,1)}, bf16[2,128,768]{2,1,0:T(8,128)(2,1)}, u32[]{:S(2)}, u32[]{:S(2)}) collective-permute-start(bf16[2,128,768]{2,1,0:T(8,128)(2,1)} %get-tuple-element.73), channel_id=1, source_target_pairs={{0,1},{1,0},{2,3},{3,2},{4,5},{5,4},{6,7},{7,6},{8,9},{9,8},{10,11... | collective-permute-start | bytes 1179656 | tf_op jit(solution)/shard_map/ppermute | solution.py:37
  4.0 23.6 %collective-permute-start.1 = (bf16[2,128,768]{2,1,0:T(8,128)(2,1)}, bf16[2,128,768]{2,1,0:T(8,128)(2,1)}, u32[]{:S(2)}, u32[]{:S(2)}) collective-permute-start(bf16[2,128,768]{2,1,0:T(8,128)(2,1)} %get-tuple-element.75), channel_id=1, source_target_pairs={{0,2},{1,3},{2,0},{3,1},{4,6},{5,7},{6,4},{7,5},{8,10},{9,11},{10,... | collective-permute-start | bytes 1179656 | tf_op jit(solution)/shard_map/ppermute | solution.py:37
  6.5 21.0 %collective-permute-start.2 = (bf16[2,128,768]{2,1,0:T(8,128)(2,1)}, bf16[2,128,768]{2,1,0:T(8,128)(2,1)}, u32[]{:S(2)}, u32[]{:S(2)}) collective-permute-start(bf16[2,128,768]{2,1,0:T(8,128)(2,1)} %get-tuple-element.74), channel_id=1, source_target_pairs={{0,3},{1,2},{2,1},{3,0},{4,7},{5,6},{6,5},{7,4},{8,11},{9,10},{10,... | collective-permute-start | bytes 1179656 | tf_op jit(solution)/shard_map/ppermute | solution.py:37
  6.8 18.1 %collective-permute-start.4 = (s32[2,128]{1,0:T(2,128)S(1)}, s32[2,128]{1,0:T(2,128)S(1)}, u32[]{:S(2)}, u32[]{:S(2)}) collective-permute-start(s32[2,128]{1,0:T(2,128)S(1)} %get-tuple-element.79), channel_id=1, source_target_pairs={{0,2},{1,3},{2,0},{3,1},{4,6},{5,7},{6,4},{7,5},{8,10},{9,11},{10,... | collective-permute-start | bytes 3080 | tf_op jit(solution)/shard_map/ppermute | solution.py:37
  13.4 13.2 %collective-permute-start.5 = (s32[2,128]{1,0:T(2,128)S(1)}, s32[2,128]{1,0:T(2,128)S(1)}, u32[]{:S(2)}, u32[]{:S(2)}) collective-permute-start(s32[2,128]{1,0:T(2,128)S(1)} %get-tuple-element.78), channel_id=1, source_target_pairs={{0,3},{1,2},{2,1},{3,0},{4,7},{5,6},{6,5},{7,4},{8,11},{9,10},{10,... | collective-permute-start | bytes 3080 | tf_op jit(solution)/shard_map/ppermute | solution.py:37
  24.9 86.3 %collective-permute-start.10 = (bf16[2,128,768]{2,1,0:T(8,128)(2,1)}, bf16[2,128,768]{2,1,0:T(8,128)(2,1)}, u32[]{:S(2)}, u32[]{:S(2)}) collective-permute-start(bf16[2,128,768]{2,1,0:T(8,128)(2,1)} %get-tuple-element.67), channel_id=1, source_target_pairs={{0,2},{1,3},{2,0},{3,1},{4,6},{5,7},{6,4},{7,5},{8,10},{9,11},{10,... | collective-permute-start | bytes 1179656 | tf_op jit(solution)/shard_map/ppermute | solution.py:37
  26.7 84.5 %collective-permute-start.11 = (bf16[2,128,768]{2,1,0:T(8,128)(2,1)}, bf16[2,128,768]{2,1,0:T(8,128)(2,1)}, u32[]{:S(2)}, u32[]{:S(2)}) collective-permute-start(bf16[2,128,768]{2,1,0:T(8,128)(2,1)} %get-tuple-element.66), channel_id=1, source_target_pairs={{0,3},{1,2},{2,1},{3,0},{4,7},{5,6},{6,5},{7,4},{8,11},{9,10},{10,... | collective-permute-start | bytes 1179656 | tf_op jit(solution)/shard_map/ppermute | solution.py:37
  27.1 84.2 %collective-permute-start.9 = (bf16[2,128,768]{2,1,0:T(8,128)(2,1)}, bf16[2,128,768]{2,1,0:T(8,128)(2,1)}, u32[]{:S(2)}, u32[]{:S(2)}) collective-permute-start(bf16[2,128,768]{2,1,0:T(8,128)(2,1)} %get-tuple-element.65), channel_id=1, source_target_pairs={{0,1},{1,0},{2,3},{3,2},{4,5},{5,4},{6,7},{7,6},{8,9},{9,8},{10,11... | collective-permute-start | bytes 1179656 | tf_op jit(solution)/shard_map/ppermute | solution.py:37
  404.7 90.5 %collective-permute-start.30 = (bf16[2,8,96,192]{3,2,1,0:T(8,128)(2,1)}, bf16[2,8,96,192]{3,2,1,0:T(8,128)(2,1)}, u32[]{:S(2)}, u32[]{:S(2)}) collective-permute-start(bf16[2,8,96,192]{3,2,1,0:T(8,128)(2,1)} %bitcast.460), channel_id=1, source_target_pairs={{0,1},{1,0},{2,3},{3,2},{4,5},{5,4},{6,7},{7,6},{8,9},{9,8},{10,11... | collective-permute-start | bytes 1769480 | tf_op jit(solution)/shard_map/ppermute | solution.py:37
  411.2 64.0 %collective-permute-start.12 = (bf16[2,128,768]{2,1,0:T(8,128)(2,1)}, bf16[2,128,768]{2,1,0:T(8,128)(2,1)}, u32[]{:S(2)}, u32[]{:S(2)}) collective-permute-start(bf16[2,128,768]{2,1,0:T(8,128)(2,1)} %get-tuple-element.62), channel_id=1, source_target_pairs={{0,1},{1,0},{2,3},{3,2},{4,5},{5,4},{6,7},{7,6},{8,9},{9,8},{10,11... | collective-permute-start | bytes 1179656 | tf_op jit(solution)/shard_map/ppermute | solution.py:37
  411.3 67.3 %collective-permute-start.13 = (bf16[2,128,768]{2,1,0:T(8,128)(2,1)}, bf16[2,128,768]{2,1,0:T(8,128)(2,1)}, u32[]{:S(2)}, u32[]{:S(2)}) collective-permute-start(bf16[2,128,768]{2,1,0:T(8,128)(2,1)} %get-tuple-element.61), channel_id=1, source_target_pairs={{0,2},{1,3},{2,0},{3,1},{4,6},{5,7},{6,4},{7,5},{8,10},{9,11},{10,... | collective-permute-start | bytes 1179656 | tf_op jit(solution)/shard_map/ppermute | solution.py:37
  412.9 67.5 %collective-permute-start.14 = (bf16[2,128,768]{2,1,0:T(8,128)(2,1)}, bf16[2,128,768]{2,1,0:T(8,128)(2,1)S(1)}, u32[]{:S(2)}, u32[]{:S(2)}) collective-permute-start(bf16[2,128,768]{2,1,0:T(8,128)(2,1)} %get-tuple-element.60), channel_id=1, source_target_pairs={{0,3},{1,2},{2,1},{3,0},{4,7},{5,6},{6,5},{7,4},{8,11},{9,10},{10,... | collective-permute-start | bytes 1179656 | tf_op jit(solution)/shard_map/ppermute | solution.py:37
  414.3 67.3 %collective-permute-start.6 = (bf16[2,128,768]{2,1,0:T(8,128)(2,1)}, bf16[2,128,768]{2,1,0:T(8,128)(2,1)}, u32[]{:S(2)}, u32[]{:S(2)}) collective-permute-start(bf16[2,128,768]{2,1,0:T(8,128)(2,1)} %get-tuple-element.70), channel_id=1, source_target_pairs={{0,1},{1,0},{2,3},{3,2},{4,5},{5,4},{6,7},{7,6},{8,9},{9,8},{10,11... | collective-permute-start | bytes 1179656 | tf_op jit(solution)/shard_map/ppermute | solution.py:37
  475.1 12.2 %collective-permute-start.7 = (bf16[2,128,768]{2,1,0:T(8,128)(2,1)}, bf16[2,128,768]{2,1,0:T(8,128)(2,1)S(1)}, u32[]{:S(2)}, u32[]{:S(2)}) collective-permute-start(bf16[2,128,768]{2,1,0:T(8,128)(2,1)} %get-tuple-element.69), channel_id=1, source_target_pairs={{0,2},{1,3},{2,0},{3,1},{4,6},{5,7},{6,4},{7,5},{8,10},{9,11},{10,... | collective-permute-start | bytes 1179656 | tf_op jit(solution)/shard_map/ppermute | solution.py:37
  478.6 15.1 %collective-permute-start.8 = (bf16[2,128,768]{2,1,0:T(8,128)(2,1)}, bf16[2,128,768]{2,1,0:T(8,128)(2,1)S(1)}, u32[]{:S(2)}, u32[]{:S(2)}) collective-permute-start(bf16[2,128,768]{2,1,0:T(8,128)(2,1)} %get-tuple-element.68), channel_id=1, source_target_pairs={{0,3},{1,2},{2,1},{3,0},{4,7},{5,6},{6,5},{7,4},{8,11},{9,10},{10,... | collective-permute-start | bytes 1179656 | tf_op jit(solution)/shard_map/ppermute | solution.py:37
  480.4 72.1 %collective-permute-start.40 = (bf16[2,8,384,192]{2,3,1,0:T(8,128)(2,1)}, bf16[2,8,384,192]{2,3,1,0:T(8,128)(2,1)S(1)}, u32[]{:S(2)}, u32[]{:S(2)}) collective-permute-start(bf16[2,8,384,192]{2,3,1,0:T(8,128)(2,1)} %slice_bitcast_fusion), channel_id=1, source_target_pairs={{0,1},{1,0},{2,3},{3,2},{4,5},{5,4},{6,7},{7,6},{8,9},{9,8},{10,11... | collective-permute-start | bytes 7077896 | tf_op jit(solution)/shard_map/ppermute | solution.py:37
  481.6 72.6 %collective-permute-start.35 = (bf16[2,8,96,768]{3,2,1,0:T(8,128)(2,1)}, bf16[2,8,96,768]{3,2,1,0:T(8,128)(2,1)S(1)}, u32[]{:S(2)}, u32[]{:S(2)}) collective-permute-start(bf16[2,8,96,768]{3,2,1,0:T(8,128)(2,1)} %slice_bitcast_fusion.2), channel_id=1, source_target_pairs={{0,1},{1,0},{2,3},{3,2},{4,5},{5,4},{6,7},{7,6},{8,9},{9,8},{10,11... | collective-permute-start | bytes 7077896 | tf_op jit(solution)/shard_map/ppermute | solution.py:37
  487.4 9.1 %collective-permute-start.25 = (bf16[2,8,96,192]{3,2,1,0:T(8,128)(2,1)S(1)}, bf16[2,8,96,192]{3,2,1,0:T(8,128)(2,1)S(1)}, u32[]{:S(2)}, u32[]{:S(2)}) collective-permute-start(bf16[2,8,96,192]{3,2,1,0:T(8,128)(2,1)S(1)} %bitcast.517), channel_id=1, source_target_pairs={{0,1},{1,0},{2,3},{3,2},{4,5},{5,4},{6,7},{7,6},{8,9},{9,8},{10,11... | collective-permute-start | bytes 1769480 | tf_op jit(solution)/shard_map/ppermute | solution.py:37
  496.5 12.0 %collective-permute-start.31 = (bf16[2,4,96,192]{3,2,1,0:T(8,128)(2,1)S(1)}, bf16[2,4,96,192]{3,2,1,0:T(8,128)(2,1)S(1)}, u32[]{:S(2)}, u32[]{:S(2)}) collective-permute-start(bf16[2,4,96,192]{3,2,1,0:T(8,128)(2,1)S(1)} %slice_bitcast_fusion.12), channel_id=1, source_target_pairs={{0,4},{4,0},{8,12},{12,8},{16,20},{20,16},{24,28},{28,24},{1,5},{5... | collective-permute-start | bytes 884744 | tf_op jit(solution)/shard_map/ppermute | solution.py:37
  496.7 20.2 %collective-permute-start.26 = (bf16[2,4,96,192]{3,2,1,0:T(8,128)(2,1)S(1)}, bf16[2,4,96,192]{3,2,1,0:T(8,128)(2,1)S(1)}, u32[]{:S(2)}, u32[]{:S(2)}) collective-permute-start(bf16[2,4,96,192]{3,2,1,0:T(8,128)(2,1)S(1)} %slice_bitcast_fusion.14), channel_id=1, source_target_pairs={{0,4},{4,0},{8,12},{12,8},{16,20},{20,16},{24,28},{28,24},{1,5},{5... | collective-permute-start | bytes 884744 | tf_op jit(solution)/shard_map/ppermute | solution.py:37
  498.9 26.4 %collective-permute-start.21 = (bf16[2,4,96,192]{3,2,1,0:T(8,128)(2,1)S(1)}, bf16[2,4,96,192]{3,2,1,0:T(8,128)(2,1)S(1)}, u32[]{:S(2)}, u32[]{:S(2)}) collective-permute-start(bf16[2,4,96,192]{3,2,1,0:T(8,128)(2,1)S(1)} %slice_bitcast_fusion.16), channel_id=1, source_target_pairs={{0,4},{4,0},{8,12},{12,8},{16,20},{20,16},{24,28},{28,24},{1,5},{5... | collective-permute-start | bytes 884744 | tf_op jit(solution)/shard_map/ppermute | solution.py:37
  508.4 24.9 %collective-permute-start.16 = (bf16[2,4,96,192]{3,2,1,0:T(8,128)(2,1)S(1)}, bf16[2,4,96,192]{3,2,1,0:T(8,128)(2,1)S(1)}, u32[]{:S(2)}, u32[]{:S(2)}) collective-permute-start(bf16[2,4,96,192]{3,2,1,0:T(8,128)(2,1)S(1)} %slice_bitcast_fusion.18), channel_id=1, source_target_pairs={{0,4},{4,0},{8,12},{12,8},{16,20},{20,16},{24,28},{28,24},{1,5},{5... | collective-permute-start | bytes 884744 | tf_op jit(solution)/shard_map/ppermute | solution.py:37
  516.9 18.1 %collective-permute-start.32 = (bf16[1,4,96,192]{3,2,1,0:T(8,128)(2,1)S(1)}, bf16[1,4,96,192]{3,2,1,0:T(8,128)(2,1)S(1)}, u32[]{:S(2)}, u32[]{:S(2)}) collective-permute-start(bf16[1,4,96,192]{3,2,1,0:T(8,128)(2,1)S(1)} %slice_bitcast_fusion.24), channel_id=1, source_target_pairs={{0,2},{1,3},{2,0},{3,1},{4,6},{5,7},{6,4},{7,5},{8,10},{9,11},{10,... | collective-permute-start | bytes 442376 | tf_op jit(solution)/shard_map/ppermute | solution.py:37
  525.3 10.3 %collective-permute-start.27 = (bf16[1,4,96,192]{3,2,1,0:T(8,128)(2,1)S(1)}, bf16[1,4,96,192]{3,2,1,0:T(8,128)(2,1)S(1)}, u32[]{:S(2)}, u32[]{:S(2)}) collective-permute-start(bf16[1,4,96,192]{3,2,1,0:T(8,128)(2,1)S(1)} %slice_bitcast_fusion.26), channel_id=1, source_target_pairs={{0,2},{1,3},{2,0},{3,1},{4,6},{5,7},{6,4},{7,5},{8,10},{9,11},{10,... | collective-permute-start | bytes 442376 | tf_op jit(solution)/shard_map/ppermute | solution.py:37
  535.0 9.1 %collective-permute-start.17 = (bf16[1,4,96,192]{3,2,1,0:T(8,128)(2,1)S(1)}, bf16[1,4,96,192]{3,2,1,0:T(8,128)(2,1)S(1)}, u32[]{:S(2)}, u32[]{:S(2)}) collective-permute-start(bf16[1,4,96,192]{3,2,1,0:T(8,128)(2,1)S(1)} %slice_bitcast_fusion.30), channel_id=1, source_target_pairs={{0,2},{1,3},{2,0},{3,1},{4,6},{5,7},{6,4},{7,5},{8,10},{9,11},{10,... | collective-permute-start | bytes 442376 | tf_op jit(solution)/shard_map/ppermute | solution.py:37
  552.5 53.5 %collective-permute-start.19 = (bf16[1,1,96,192]{3,2,1,0:T(8,128)(2,1)S(1)}, bf16[1,1,96,192]{3,2,1,0:T(8,128)(2,1)S(1)}, u32[]{:S(2)}, u32[]{:S(2)}) collective-permute-start(bf16[1,1,96,192]{3,2,1,0:T(8,128)(2,1)S(1)} %slice_bitcast_fusion.50), channel_id=1, source_target_pairs={{0,16},{4,20},{8,24},{12,28},{16,0},{20,4},{24,8},{28,12},{1,17},{... | collective-permute-start | bytes 110600 | tf_op jit(solution)/shard_map/ppermute | solution.py:37
  554.2 29.0 %collective-permute-start.41 = (bf16[2,4,384,192]{2,3,1,0:T(8,128)(2,1)S(1)}, bf16[2,4,384,192]{2,3,1,0:T(8,128)(2,1)S(1)}, u32[]{:S(2)}, u32[]{:S(2)}) collective-permute-start(bf16[2,4,384,192]{2,3,1,0:T(8,128)(2,1)S(1)} %slice_bitcast_fusion.4), channel_id=1, source_target_pairs={{0,4},{4,0},{8,12},{12,8},{16,20},{20,16},{24,28},{28,24},{1,5},{5... | collective-permute-start | bytes 3538952 | tf_op jit(solution)/shard_map/ppermute | solution.py:37
  555.1 49.1 %collective-permute-start.36 = (bf16[2,4,96,768]{3,2,1,0:T(8,128)(2,1)S(1)}, bf16[2,4,96,768]{3,2,1,0:T(8,128)(2,1)S(1)}, u32[]{:S(2)}, u32[]{:S(2)}) collective-permute-start(bf16[2,4,96,768]{3,2,1,0:T(8,128)(2,1)S(1)} %slice_bitcast_fusion.6), channel_id=1, source_target_pairs={{0,4},{4,0},{8,12},{12,8},{16,20},{20,16},{24,28},{28,24},{1,5},{5... | collective-permute-start | bytes 3538952 | tf_op jit(solution)/shard_map/ppermute | solution.py:37
  583.4 23.3 %collective-permute-start.42 = (bf16[1,4,384,192]{2,3,1,0:T(8,128)(2,1)S(1)}, bf16[1,4,384,192]{2,3,1,0:T(8,128)(2,1)S(1)}, u32[]{:S(2)}, u32[]{:S(2)}) collective-permute-start(bf16[1,4,384,192]{2,3,1,0:T(8,128)(2,1)S(1)} %slice_bitcast_fusion.8), channel_id=1, source_target_pairs={{0,2},{1,3},{2,0},{3,1},{4,6},{5,7},{6,4},{7,5},{8,10},{9,11},{10,... | collective-permute-start | bytes 1769480 | tf_op jit(solution)/shard_map/ppermute | solution.py:37
  604.4 11.2 %collective-permute-start.37 = (bf16[1,4,96,768]{3,2,1,0:T(8,128)(2,1)S(1)}, bf16[1,4,96,768]{3,2,1,0:T(8,128)(2,1)S(1)}, u32[]{:S(2)}, u32[]{:S(2)}) collective-permute-start(bf16[1,4,96,768]{3,2,1,0:T(8,128)(2,1)S(1)} %slice_bitcast_fusion.10), channel_id=1, source_target_pairs={{0,2},{1,3},{2,0},{3,1},{4,6},{5,7},{6,4},{7,5},{8,10},{9,11},{10,... | collective-permute-start | bytes 1769480 | tf_op jit(solution)/shard_map/ppermute | solution.py:37
  606.8 10.5 %collective-permute-start.43 = (bf16[1,2,384,192]{2,3,1,0:T(8,128)(2,1)S(1)}, bf16[1,2,384,192]{2,3,1,0:T(8,128)(2,1)S(1)}, u32[]{:S(2)}, u32[]{:S(2)}) collective-permute-start(bf16[1,2,384,192]{2,3,1,0:T(8,128)(2,1)S(1)} %slice_bitcast_fusion.20), channel_id=1, source_target_pairs={{0,8},{4,12},{8,0},{12,4},{16,24},{20,28},{24,16},{28,20},{1,9},{5... | collective-permute-start | bytes 884744 | tf_op jit(solution)/shard_map/ppermute | solution.py:37
  617.4 10.4 %collective-permute-start.44 = (bf16[1,1,384,192]{2,3,1,0:T(8,128)(2,1)S(1)}, bf16[1,1,384,192]{2,3,1,0:T(8,128)(2,1)S(1)}, u32[]{:S(2)}, u32[]{:S(2)}) collective-permute-start(bf16[1,1,384,192]{2,3,1,0:T(8,128)(2,1)S(1)} %slice_bitcast_fusion.32), channel_id=1, source_target_pairs={{0,16},{4,20},{8,24},{12,28},{16,0},{20,4},{24,8},{28,12},{1,17},{... | collective-permute-start | bytes 442376 | tf_op jit(solution)/shard_map/ppermute | solution.py:37
  (73 other events, 671.1 us)
